TPU v7x, 128 devices: a whole 4x4x4 slice. The times are simulated.
128 devices in a mesh: row: 16 (over y, z), col: 8 (over x, core).
Axes of the slice: x: 4, y: 4, z: 4, core: 2. Of those that a mesh axis runs over, the one named last changes fastest.
Arguments:
- spectrum_noise: float32 [2, 8192, 8192], P(None, ('row', 'col')), may hold values from -6 to 6
- power_spectrum: float32 [8192, 8192], P(('row', 'col')), may hold values from 0.1 to 10
- site_block: int32 [16384], P(('row', 'col')), may hold values from 0 to 127, as said below
- site_cell: int32 [2, 16384], P(None, ('row', 'col')), may hold values from 0 to 8191, as said below
- site_frac: float32 [2, 16384], P(None, ('row', 'col')), may hold values from 0 to 1
Outputs:
- field: float32 [2, 8192, 8192], P(None, ('row', 'col'))
- samples: float32 [2, 16384], P(None, ('row', 'col'))
Inputs may be any that keep to these rules, and one draw needn't show every extreme that they name: `site_block`: no row block holds more than 2 stations of one device, and every device has exactly 2 stations in some block. Every row block holds a station of the device of the same index, in the block's last row. `site_cell`: the first row is below 64.
All inputs are finite; a program needn't handle non-finite values.
Results may differ from a plain program's by a relative error of at most 0.00008.
Values sent between devices are 32-bit elements; how exact they have to be, the bound alone decides.
No kernel may reach another device: no remote copies, remote signals or barrier semaphores. Data moves between devices by JAX's collectives and lax.ppermute only.
A program may use at most 128 MiB of HBM per device.

v0:
```python
import numpy as np
import ml_dtypes
import jax
import jax.numpy as jnp
from jax import lax
from jax.experimental import pallas as pl
from jax.experimental.pallas import tpu as pltpu
from jax.sharding import PartitionSpec as P

GRID = 8192
DEVICES = 128
ROWS = 64
MESSAGE = 65
AXES = ("row", "col")
VMEM = pl.BlockSpec(memory_space=pltpu.VMEM)
HIGH = lax.Precision.HIGHEST
LAST = (((1,), (1,)), ((), ()))


def phase(product, length):
    angle = 2.0 * np.pi / length * (product % length)
    return np.cos(angle), np.sin(angle)


def complex_matrix(cosine, sine):
    return np.block([[cosine, -sine], [sine, cosine]])


def split_table(table):
    high = table.astype(ml_dtypes.bfloat16)
    low = (table - high.astype(np.float64)).astype(ml_dtypes.bfloat16)
    return high, low


def make_tables():
    short, long = np.arange(64), np.arange(128)
    high, low = split_table(complex_matrix(*phase(np.outer(short, short), 64)))
    short_first = np.block([[high, high], [low, np.zeros_like(low)]])
    turn_first = np.stack(phase(np.outer(short, long), GRID)).astype(np.float32)
    long_both = np.stack(split_table(complex_matrix(*phase(np.outer(long, long), 128))))
    turn_second = np.stack(phase(np.outer(long, short), GRID)) / GRID
    turn_second = np.concatenate([turn_second, turn_second], axis=2).astype(np.float32)
    cosine, sine = phase(np.outer(short, short), 64)
    pair = np.eye(2)
    short_second = np.stack(
        split_table(complex_matrix(np.kron(pair, cosine), np.kron(pair, sine)))
    )
    return short_first, turn_first, long_both, turn_second, short_second


def split(value):
    high = value.astype(jnp.bfloat16)
    low = (value - high.astype(jnp.float32)).astype(jnp.bfloat16)
    return high, low


def dot(left, right, dims=(((1,), (0,)), ((), ()))):
    return lax.dot_general(left, right, dims, preferred_element_type=jnp.float32)


def split_dot(table, value, dims=(((1,), (0,)), ((), ()))):
    high, low = split(value)
    return dot(table[0], high, dims) + dot(table[0], low, dims) + dot(table[1], high, dims)


def site_slots(block):
    wide = jnp.broadcast_to(block.astype(jnp.float32), (DEVICES, DEVICES))
    before = lax.broadcasted_iota(jnp.int32, (DEVICES, DEVICES), 0)
    after = lax.broadcasted_iota(jnp.int32, (DEVICES, DEVICES), 1)
    earlier = (wide == wide.T) & (before < after)
    return jnp.sum(jnp.where(earlier, 1.0, 0.0), axis=0, keepdims=True)


def site_requests(block, cell, frac):
    slot = site_slots(block)
    row, column = cell[0:1], cell[1:2]
    column_next = (column + 1) & (GRID - 1)
    part_row, part_col = frac[0:1], frac[1:2]
    edge = row == ROWS - 1
    row_next = jnp.where(edge, row, row + 1)

    def line(field_row, field_col):
        return ((field_row >> 3) * 512 + (field_col >> 7) * 8 + (field_row & 7)).astype(jnp.float32)

    lane = (column & 127).astype(jnp.float32)
    lane_next = (column_next & 127).astype(jnp.float32)
    lower = jnp.where(edge, 0.0, part_row)
    zero = jnp.zeros_like(row)
    own = [
        line(row, column),
        line(row, column_next),
        line(row_next, column),
        line(row_next, column_next),
        lane,
        lane_next,
        (1 - part_row) * (1 - part_col),
        (1 - part_row) * part_col,
        lower * (1 - part_col),
        lower * part_col,
    ]
    halo = [
        line(zero, column),
        line(zero, column_next),
        lane,
        lane_next,
        part_row * (1 - part_col),
        part_row * part_col,
    ]
    blank = jnp.zeros((1, DEVICES), jnp.float32)
    groups = []
    for at, values in ((0, own), (10, own), (20, halo), (26, halo)):
        lines = [blank] * at + values
        groups.append(jnp.concatenate(lines + [blank] * (DEVICES - len(lines)), axis=0))
    owner = lax.broadcasted_iota(jnp.int32, (DEVICES, DEVICES), 0)
    here = owner == block
    below = (owner == ((block + 1) & (DEVICES - 1))) & edge
    picks = []
    for mask in (here, below):
        for which in (0.0, 1.0):
            picks.append(jnp.where(mask & (slot == which), 1.0, 0.0))
    return lax.dot_general(
        jnp.concatenate(picks, axis=1),
        jnp.concatenate(groups, axis=1),
        LAST,
        precision=HIGH,
        preferred_element_type=jnp.float32,
    )


def first_kernel(
    noise_hbm,
    power_hbm,
    block_ref,
    cell_ref,
    frac_ref,
    short_ref,
    turn_ref,
    long_ref,
    out_ref,
    noise,
    power,
    middle,
    noise_sem,
    power_sem,
):
    copies = []
    for i in range(8):
        copies.append(
            (
                pltpu.make_async_copy(noise_hbm.at[:, i], noise.at[:, i], noise_sem.at[i]),
                pltpu.make_async_copy(power_hbm.at[i], power.at[i], power_sem.at[i]),
            )
        )
        copies[-1][0].start()
        copies[-1][1].start()
    out_ref[pl.ds(MESSAGE - 1, DEVICES, stride=MESSAGE), :] = site_requests(
        block_ref[...], cell_ref[...], frac_ref[...]
    )
    for i in range(8):
        copies[i][0].wait()
        copies[i][1].wait()

        def rows(pair, carry, i=i):
            parts = []
            for k in range(2):
                at = pl.ds(2 * pair + k, 64, stride=8)
                amplitude = jnp.sqrt(power[i, at, :])
                stacked = jnp.concatenate(
                    [amplitude * noise[0, i, at, :], amplitude * noise[1, i, at, :]], axis=0
                )
                parts.append(jnp.concatenate(split(stacked), axis=0))
            sums = dot(short_ref[...], jnp.concatenate(parts, axis=1))
            sums = sums[:128] + sums[128:]
            for k in range(2):
                real = sums[:64, 128 * k : 128 * k + 128]
                imag = sums[64:, 128 * k : 128 * k + 128]
                at = pl.ds(8 * i + 2 * pair + k, 64, stride=64)
                middle[0, at, :] = real * turn_ref[0] - imag * turn_ref[1]
                middle[1, at, :] = real * turn_ref[1] + imag * turn_ref[0]
            return carry

        lax.fori_loop(0, 4, rows, 0, unroll=True)

    def columns(step, carry):
        at = pl.ds(pl.multiple_of(256 * step, 256), 256)
        value = jnp.concatenate([middle[0, at, :], middle[1, at, :]], axis=1)
        sums = split_dot(long_ref, value, LAST)
        for part in range(2):
            for k in range(2):
                j = 32 * part + 2 * step + k
                out_ref[pl.ds(j, DEVICES, stride=MESSAGE), :] = sums[
                    128 * part : 128 * part + 128, 128 * k : 128 * k + 128
                ]
        return carry

    lax.fori_loop(0, 16, columns, 0, unroll=4)


def second_kernel(
    got_ref,
    long_ref,
    turn_ref,
    short_ref,
    field_hbm,
    answer_ref,
    field,
    picked,
    code_vmem,
    code_smem,
    field_sem,
    code_sem,
):
    asked = got_ref[pl.ds(MESSAGE - 1, DEVICES, stride=MESSAGE), :]
    code_vmem[...] = (asked + 0.5).astype(jnp.int32)
    code_copy = pltpu.make_async_copy(code_vmem, code_smem, code_sem)
    code_copy.start()
    copies = []
    for i in range(8):
        for half in range(2):
            pair = 4 * i + 2 * half
            value = jnp.concatenate(
                [
                    jnp.concatenate(
                        [
                            got_ref[pl.ds(32 * part + pair + k, DEVICES, stride=MESSAGE), :]
                            for k in range(2)
                        ],
                        axis=1,
                    )
                    for part in range(2)
                ],
                axis=0,
            )
            sums = split_dot(long_ref, value)
            turned = []
            for k in range(2):
                real = sums[:128, 128 * k : 128 * k + 128]
                imag = sums[128:, 128 * k : 128 * k + 128]
                turned.append(
                    jnp.concatenate(
                        [
                            real * turn_ref[0] - imag * turn_ref[1],
                            real * turn_ref[1] + imag * turn_ref[0],
                        ],
                        axis=1,
                    )
                )
            sums = split_dot(short_ref, jnp.concatenate(turned, axis=0), LAST)
            for part in range(2):
                for odd in range(2):
                    for k in range(2):
                        top = 128 * part + 64 * odd
                        at = pl.ds(512 * i + 4 * half + 2 * k + odd, 64, stride=8)
                        field[part, at, :] = sums[top : top + 64, 128 * k : 128 * k + 128]
        span = pl.ds(512 * i, 512)
        copies.append(
            pltpu.make_async_copy(field.at[:, span], field_hbm.at[:, span], field_sem.at[i])
        )
        copies[-1].start()
    code_copy.wait()

    def gather(device, carry):
        for which in range(2):
            for k in range(6):
                lane = 10 * which + k if k < 4 else 20 + 6 * which + k - 4
                line = code_smem[device, lane]
                for part in range(2):
                    picked[which, part, k, pl.ds(device, 1), :] = field[part, pl.ds(line, 1), :]
        return carry

    lax.fori_loop(0, DEVICES, gather, 0, unroll=4)
    lanes = lax.broadcasted_iota(jnp.int32, (DEVICES, 128), 1).astype(jnp.float32)
    answer = jnp.zeros((DEVICES, 128), jnp.float32)
    for which in range(2):
        own, halo = 10 * which, 20 + 6 * which

        def column(at):
            return asked[:, at : at + 1]

        first = lanes == column(own + 4)
        second = lanes == column(own + 5)
        halo_first = lanes == column(halo + 2)
        halo_second = lanes == column(halo + 3)
        for part in range(2):
            left = column(own + 6) * picked[which, part, 0] + column(own + 8) * picked[which, part, 2]
            right = column(own + 7) * picked[which, part, 1] + column(own + 9) * picked[which, part, 3]
            value = jnp.where(first, left, 0.0) + jnp.where(second, right, 0.0)
            edge = jnp.where(halo_first, column(halo + 4) * picked[which, part, 4], 0.0)
            edge += jnp.where(halo_second, column(halo + 5) * picked[which, part, 5], 0.0)
            answer = jnp.where(
                lanes == 2 * which + part, jnp.sum(value, axis=1, keepdims=True), answer
            )
            answer = jnp.where(
                lanes == 4 + 2 * which + part, jnp.sum(edge, axis=1, keepdims=True), answer
            )
    answer_ref[...] = answer
    for copy in copies:
        copy.wait()


def last_kernel(answer_ref, block_ref, cell_ref, out_ref):
    block = block_ref[...]
    slot = site_slots(block)
    edge = cell_ref[0:1] == ROWS - 1
    owner = lax.broadcasted_iota(jnp.int32, (DEVICES, DEVICES), 0)
    values = answer_ref[...].T[:8]

    def pick(mask):
        return jnp.dot(
            values,
            jnp.where(mask, 1.0, 0.0),
            precision=HIGH,
            preferred_element_type=jnp.float32,
        )

    here = pick(owner == block)
    below = pick(owner == ((block + 1) & (DEVICES - 1)))
    own = jnp.where(slot == 0.0, here[0:2], here[2:4])
    halo = jnp.where(slot == 0.0, below[4:6], below[6:8])
    out_ref[...] = own + jnp.where(edge, halo, 0.0)


def exchange(value):
    return lax.all_to_all(value, AXES, split_axis=0, concat_axis=0, tiled=True)


def per_device(spectrum_noise, power_spectrum, site_block, site_cell, site_frac):
    short_first, turn_first, long_both, turn_second, short_second = make_tables()
    any_space = pl.BlockSpec(memory_space=pl.ANY)
    noise = spectrum_noise.reshape(2, 8, 8, 64, 128).transpose(0, 1, 3, 2, 4).reshape(2, 8, 512, 128)
    power = power_spectrum.reshape(8, 8, 64, 128).transpose(0, 2, 1, 3).reshape(8, 512, 128)
    block = site_block.reshape(1, DEVICES)
    sent = pl.pallas_call(
        first_kernel,
        out_shape=jax.ShapeDtypeStruct((DEVICES * MESSAGE, 128), jnp.float32),
        in_specs=[any_space, any_space] + [VMEM] * 6,
        out_specs=VMEM,
        scratch_shapes=[
            pltpu.VMEM((2, 8, 512, 128), jnp.float32),
            pltpu.VMEM((8, 512, 128), jnp.float32),
            pltpu.VMEM((2, 4096, 128), jnp.float32),
            pltpu.SemaphoreType.DMA((8,)),
            pltpu.SemaphoreType.DMA((8,)),
        ],
        compiler_params=pltpu.CompilerParams(vmem_limit_bytes=40 << 20),
        name="first_pass",
    )(noise, power, block, site_cell, site_frac, short_first, turn_first, long_both)
    got = exchange(sent.reshape(DEVICES * MESSAGE, 1, 128)).reshape(DEVICES * MESSAGE, 128)
    field, answer = pl.pallas_call(
        second_kernel,
        out_shape=(
            jax.ShapeDtypeStruct((2, 4096, 128), jnp.float32),
            jax.ShapeDtypeStruct((DEVICES, 128), jnp.float32),
        ),
        in_specs=[VMEM] * 4,
        out_specs=(any_space, VMEM),
        scratch_shapes=[
            pltpu.VMEM((2, 4096, 128), jnp.float32),
            pltpu.VMEM((2, 2, 6, DEVICES, 128), jnp.float32),
            pltpu.VMEM((DEVICES, 128), jnp.int32),
            pltpu.SMEM((DEVICES, 128), jnp.int32),
            pltpu.SemaphoreType.DMA((8,)),
            pltpu.SemaphoreType.DMA,
        ],
        compiler_params=pltpu.CompilerParams(vmem_limit_bytes=40 << 20),
        name="second_pass",
    )(got, long_both, turn_second, short_second)
    back = exchange(answer.reshape(DEVICES, 1, 128)).reshape(DEVICES, 128)
    samples = pl.pallas_call(
        last_kernel,
        out_shape=jax.ShapeDtypeStruct((2, DEVICES), jnp.float32),
        in_specs=[VMEM] * 3,
        out_specs=VMEM,
        name="samples",
    )(back, block, site_cell)
    field = field.reshape(2, 8, 64, 8, 128).transpose(0, 1, 3, 2, 4).reshape(2, ROWS, GRID)
    return field, samples


def solution(mesh):
    return jax.shard_map(
        per_device,
        mesh=mesh,
        in_specs=(
            P(None, AXES, None),
            P(AXES, None),
            P(AXES),
            P(None, AXES),
            P(None, AXES),
        ),
        out_specs=(P(None, AXES, None), P(None, AXES)),
        check_vma=False,
    )
```

profile of v0, /device:TPU:1, one launch (start us, length us, event | category | flops | bytes accessed | tf_op | source)
XLA Modules:
  0.0 108.0 jit_solution(1529741244845531931)
XLA Ops:
  0.6 0.0 copy-start
  0.6 2.2 %copy-done = f32[2,64,8192]{2,1,0:T(8,128)S(1)} copy-done((f32[2,64,8192]{2,1,0:T(8,128)S(1)}, f32[2,64,8192]{2,1,0:T(8,128)}, u32[]{:S(2)}) %copy-start) | copy-done | bytes 4194328
  2.8 0.0 copy-start.1
  2.8 1.6 %copy-done.1 = f32[64,8192]{1,0:T(8,128)S(1)} copy-done((f32[64,8192]{1,0:T(8,128)S(1)}, f32[64,8192]{1,0:T(8,128)}, u32[]{:S(2)}) %copy-start.1) | copy-done | bytes 2097176
  4.4 0.0 copy-start.2
  4.4 0.9 copy-done.2
  5.4 0.0 copy-start.4
  5.4 0.9 copy-done.4
  6.3 0.0 copy-start.6
  6.3 0.8 copy-done.6
  7.1 0.0 copy-start.7
  7.1 0.7 copy-done.7
  7.8 0.0 copy-start.8
  7.8 0.7 copy-done.8
  8.4 0.7 copy-done.9
  9.1 9.5 %first_pass.1 = f32[8320,128]{1,0:T(8,128)S(1)} custom-call(f32[2,8,512,128]{3,2,1,0:T(8,128)S(1)} %bitcast.26, f32[8,512,128]{2,1,0:T(8,128)S(1)} %bitcast.27, s32[1,128]{1,0:T(1,128)S(1)} %bitcast.30, s32[2,128]{1,0:T(2,128)S(1)} %copy-done.7, f32[2,128]{1,0:T(2,128)S(1)} %copy-done.9, bf16[256,256]{1,0:T(8,128)(2,1)S(1)} %copy-done.4, ...), custom_call_target="tpu_custom_call" | custom-call | tf_op jit(solution)/shard_map/first_pass/pallas_call | solution.py:333
  18.6 0.0 copy-start.3
  18.7 0.0 copy-start.5
  18.7 65.3 %all_to_all.10 = f32[8320,1,128]{2,1,0:T(1,128)S(1)} all-to-all(f32[8320,1,128]{2,1,0:T(1,128)S(1)} %bitcast.25), channel_id=1, replica_groups=mesh['row'=16,'col'=8] {'row','col'}, dimensions={0} | all-to-all | bytes 8519680 | tf_op jit(solution)/shard_map/all_to_all | solution.py:324
  84.0 0.0 copy-done.3
  84.0 0.0 copy-done.5
  84.0 8.0 %second_pass.1 = (f32[2,4096,128]{2,1,0:T(8,128)}, f32[128,128]{1,0:T(8,128)S(1)}) custom-call(f32[8320,128]{1,0:T(8,128)S(1)} %bitcast.24, bf16[2,256,256]{2,1,0:T(8,128)(2,1)S(1)} %copy-done.2, f32[2,128,128]{2,1,0:T(8,128)S(1)} %copy-done.5, bf16[2,256,256]{2,1,0:T(8,128)(2,1)S(1)} %copy-done.3), custom_call_target="tpu_custom_call" | custom-call | tf_op jit(solution)/shard_map/second_pass/pallas_call | solution.py:349
  92.0 14.4 %all_to_all.11 = f32[128,1,128]{2,1,0:T(1,128)} all-to-all(f32[128,1,128]{2,1,0:T(1,128)S(1)} %bitcast.28), channel_id=1, replica_groups=mesh['row'=16,'col'=8] {'row','col'}, dimensions={0} | all-to-all | bytes 131072 | tf_op jit(solution)/shard_map/all_to_all | solution.py:324
  106.3 1.7 %samples.1 = f32[2,128]{1,0:T(2,128)} custom-call(f32[128,128]{1,0:T(8,128)} %bitcast.31, s32[1,128]{1,0:T(1,128)} %bitcast.29, s32[2,128]{1,0:T(2,128)} %cell_ref.3), custom_call_target="tpu_custom_call" | custom-call | tf_op jit(solution)/shard_map/samples/pallas_call | solution.py:369
  (1 shorter events, 0.0 us)
Async XLA Ops:
  0.6 2.2 %copy-start = (f32[2,64,8192]{2,1,0:T(8,128)S(1)}, f32[2,64,8192]{2,1,0:T(8,128)}, u32[]{:S(2)}) copy-start(f32[2,64,8192]{2,1,0:T(8,128)} %param.10) | copy-start | bytes 12582916
  2.8 1.6 %copy-start.1 = (f32[64,8192]{1,0:T(8,128)S(1)}, f32[64,8192]{1,0:T(8,128)}, u32[]{:S(2)}) copy-start(f32[64,8192]{1,0:T(8,128)} %param.11) | copy-start | bytes 6291460
  4.4 0.9 copy-start.2
  5.4 0.9 copy-start.4
  6.3 0.8 copy-start.6
  7.1 0.7 copy-start.7
  7.8 0.7 copy-start.8
  8.4 0.7 copy-start.9
  18.6 65.3 %copy-start.3 = (bf16[2,256,256]{2,1,0:T(8,128)(2,1)S(1)}, bf16[2,256,256]{2,1,0:T(8,128)(2,1)}, u32[]{:S(2)}) copy-start(bf16[2,256,256]{2,1,0:T(8,128)(2,1)} %constant.14.clone.short_ref) | copy-start | bytes 786436
  18.7 65.3 %copy-start.5 = (f32[2,128,128]{2,1,0:T(8,128)S(1)}, f32[2,128,128]{2,1,0:T(8,128)}, u32[]{:S(2)}) copy-start(f32[2,128,128]{2,1,0:T(8,128)} %constant.13.clone.turn_ref) | copy-start | bytes 393220
where the time goes:
time: 108 us
  blocking collectives  79.7 us (74%)
  Pallas kernels  19.2 us (18%)
  local copies, waits for them, and re-layouts  8.49 us (8%)
    all_to_all x2, blocking collectives, exchange(): return lax.all_to_all(value, AXES, split_axis=0, concat_axis=0, tiled=True)  79.7 us
    pallas_call x1, Pallas kernels, per_device(): pl.pallas_call(first_kernel, out_shape=jax.ShapeDtypeStruct((DEVICES * ME...  9.51 us
    unnamed x20, local copies, waits for them, and re-layouts  8.49 us
    pallas_call x1, Pallas kernels, per_device(): pl.pallas_call(second_kernel, out_shape=(jax.ShapeDtypeStruct((2, 4096, 1...  7.98 us

commit v1 on v0

--- a/solution.py
+++ b/solution.py
@@ -11,6 +11,8 @@
 DEVICES = 128
 ROWS = 64
 MESSAGE = 65
+PITCH = 72
+CHUNKS = ((0, 1), (1, 1), (2, 2), (4, 4))
 AXES = ("row", "col")
 VMEM = pl.BlockSpec(memory_space=pltpu.VMEM)
 HIGH = lax.Precision.HIGHEST
@@ -130,60 +132,93 @@
 def first_kernel(
     noise_hbm,
     power_hbm,
+    block_hbm,
+    cell_hbm,
+    frac_hbm,
+    short_hbm,
+    turn_hbm,
+    long_hbm,
+    out_ref,
+    noise,
+    power,
     block_ref,
     cell_ref,
     frac_ref,
     short_ref,
     turn_ref,
     long_ref,
-    out_ref,
-    noise,
-    power,
     middle,
     noise_sem,
     power_sem,
+    small_sem,
 ):
-    copies = []
-    for i in range(8):
-        copies.append(
+    small = [
+        pltpu.make_async_copy(source, target, small_sem.at[k])
+        for k, (source, target) in enumerate(
             (
-                pltpu.make_async_copy(noise_hbm.at[:, i], noise.at[:, i], noise_sem.at[i]),
-                pltpu.make_async_copy(power_hbm.at[i], power.at[i], power_sem.at[i]),
+                (block_hbm, block_ref),
+                (cell_hbm, cell_ref),
+                (frac_hbm, frac_ref),
+                (short_hbm, short_ref),
+                (turn_hbm, turn_ref),
+                (long_hbm, long_ref),
             )
         )
-        copies[-1][0].start()
-        copies[-1][1].start()
+    ]
+    large = []
+    for k, (start, count) in enumerate(CHUNKS):
+        span = pl.ds(start, count)
+        large.append(
+            (
+                pltpu.make_async_copy(power_hbm.at[span], power.at[span], power_sem.at[k]),
+                pltpu.make_async_copy(noise_hbm.at[:, span], noise.at[:, span], noise_sem.at[k]),
+            )
+        )
+    for copy in small[:5] + list(large[0]) + small[5:]:
+        copy.start()
+    for pair in large[1:]:
+        pair[0].start()
+        pair[1].start()
+    for copy in small[:3]:
+        copy.wait()
     out_ref[pl.ds(MESSAGE - 1, DEVICES, stride=MESSAGE), :] = site_requests(
         block_ref[...], cell_ref[...], frac_ref[...]
     )
-    for i in range(8):
-        copies[i][0].wait()
-        copies[i][1].wait()
-
-        def rows(pair, carry, i=i):
+    small[3].wait()
+    small[4].wait()
+    for k, (start, count) in enumerate(CHUNKS):
+        large[k][0].wait()
+        large[k][1].wait()
+        for first in range(8 * start, 8 * (start + count), 2):
             parts = []
-            for k in range(2):
-                at = pl.ds(2 * pair + k, 64, stride=8)
-                amplitude = jnp.sqrt(power[i, at, :])
+            for row in (first, first + 1):
+                at = pl.ds(row % 8, 64, stride=8)
+                level = power[row // 8, at, :]
+                amplitude = level * lax.rsqrt(level)
                 stacked = jnp.concatenate(
-                    [amplitude * noise[0, i, at, :], amplitude * noise[1, i, at, :]], axis=0
+                    [amplitude * noise[0, row // 8, at, :], amplitude * noise[1, row // 8, at, :]],
+                    axis=0,
                 )
                 parts.append(jnp.concatenate(split(stacked), axis=0))
             sums = dot(short_ref[...], jnp.concatenate(parts, axis=1))
             sums = sums[:128] + sums[128:]
-            for k in range(2):
-                real = sums[:64, 128 * k : 128 * k + 128]
-                imag = sums[64:, 128 * k : 128 * k + 128]
-                at = pl.ds(8 * i + 2 * pair + k, 64, stride=64)
+            for k2 in range(2):
+                real = sums[:64, 128 * k2 : 128 * k2 + 128]
+                imag = sums[64:, 128 * k2 : 128 * k2 + 128]
+                at = pl.ds(first + k2, 64, stride=PITCH)
                 middle[0, at, :] = real * turn_ref[0] - imag * turn_ref[1]
                 middle[1, at, :] = real * turn_ref[1] + imag * turn_ref[0]
-            return carry
-
-        lax.fori_loop(0, 4, rows, 0, unroll=True)
-
-    def columns(step, carry):
-        at = pl.ds(pl.multiple_of(256 * step, 256), 256)
-        value = jnp.concatenate([middle[0, at, :], middle[1, at, :]], axis=1)
+    small[5].wait()
+    for step in range(16):
+        value = jnp.concatenate(
+            [
+                jnp.concatenate(
+                    [middle[part, pl.ds(PITCH * (4 * step + k), 64), :] for k in range(4)], axis=0
+                )
+                for part in range(2)
+            ],
+            axis=1,
+        )
         sums = split_dot(long_ref, value, LAST)
         for part in range(2):
             for k in range(2):
@@ -191,9 +226,6 @@
                 out_ref[pl.ds(j, DEVICES, stride=MESSAGE), :] = sums[
                     128 * part : 128 * part + 128, 128 * k : 128 * k + 128
                 ]
-        return carry
-
-    lax.fori_loop(0, 16, columns, 0, unroll=4)
 
 
 def second_kernel(
@@ -259,40 +291,47 @@
         copies[-1].start()
     code_copy.wait()
 
+    head = lax.broadcasted_iota(jnp.int32, (1, 128), 1) == 0
+
     def gather(device, carry):
         for which in range(2):
-            for k in range(6):
-                lane = 10 * which + k if k < 4 else 20 + 6 * which + k - 4
+            for k in range(3):
+                lane = 10 * which + 2 * k if k < 2 else 20 + 6 * which
                 line = code_smem[device, lane]
+                line_next = code_smem[device, lane + 1]
                 for part in range(2):
-                    picked[which, part, k, pl.ds(device, 1), :] = field[part, pl.ds(line, 1), :]
+                    picked[which, part, k, pl.ds(device, 1), :] = jnp.where(
+                        head,
+                        field[part, pl.ds(line_next, 1), :],
+                        field[part, pl.ds(line, 1), :],
+                    )
         return carry
 
-    lax.fori_loop(0, DEVICES, gather, 0, unroll=4)
+    lax.fori_loop(0, DEVICES, gather, 0, unroll=8)
     lanes = lax.broadcasted_iota(jnp.int32, (DEVICES, 128), 1).astype(jnp.float32)
     answer = jnp.zeros((DEVICES, 128), jnp.float32)
+
+    def column(at):
+        return asked[:, at : at + 1]
+
     for which in range(2):
         own, halo = 10 * which, 20 + 6 * which
 
-        def column(at):
-            return asked[:, at : at + 1]
-
-        first = lanes == column(own + 4)
-        second = lanes == column(own + 5)
-        halo_first = lanes == column(halo + 2)
-        halo_second = lanes == column(halo + 3)
+        def weights(lane, weight):
+            return jnp.where(lanes == column(lane), column(weight), 0.0) + jnp.where(
+                lanes == column(lane + 1), column(weight + 1), 0.0
+            )
+
+        upper = weights(own + 4, own + 6)
+        lower = weights(own + 4, own + 8)
+        edge = weights(halo + 2, halo + 4)
         for part in range(2):
-            left = column(own + 6) * picked[which, part, 0] + column(own + 8) * picked[which, part, 2]
-            right = column(own + 7) * picked[which, part, 1] + column(own + 9) * picked[which, part, 3]
-            value = jnp.where(first, left, 0.0) + jnp.where(second, right, 0.0)
-            edge = jnp.where(halo_first, column(halo + 4) * picked[which, part, 4], 0.0)
-            edge += jnp.where(halo_second, column(halo + 5) * picked[which, part, 5], 0.0)
+            value = upper * picked[which, part, 0] + lower * picked[which, part, 1]
             answer = jnp.where(
                 lanes == 2 * which + part, jnp.sum(value, axis=1, keepdims=True), answer
             )
-            answer = jnp.where(
-                lanes == 4 + 2 * which + part, jnp.sum(edge, axis=1, keepdims=True), answer
-            )
+            beyond = jnp.sum(edge * picked[which, part, 2], axis=1, keepdims=True)
+            answer = jnp.where(lanes == 4 + 2 * which + part, beyond, answer)
     answer_ref[...] = answer
     for copy in copies:
         copy.wait()
@@ -304,17 +343,13 @@
     edge = cell_ref[0:1] == ROWS - 1
     owner = lax.broadcasted_iota(jnp.int32, (DEVICES, DEVICES), 0)
     values = answer_ref[...].T[:8]
-
-    def pick(mask):
-        return jnp.dot(
-            values,
-            jnp.where(mask, 1.0, 0.0),
-            precision=HIGH,
-            preferred_element_type=jnp.float32,
-        )
-
-    here = pick(owner == block)
-    below = pick(owner == ((block + 1) & (DEVICES - 1)))
+    masks = jnp.concatenate([owner == block, owner == ((block + 1) & (DEVICES - 1))], axis=1)
+    high, middle = split(values)
+    rest = values - high.astype(jnp.float32) - middle.astype(jnp.float32)
+    terms = jnp.concatenate([high, middle, rest.astype(jnp.bfloat16)], axis=0)
+    sums = dot(terms, jnp.where(masks, 1.0, 0.0).astype(jnp.bfloat16))
+    sums = sums[0:8] + sums[8:16] + sums[16:24]
+    here, below = sums[:, :DEVICES], sums[:, DEVICES:]
     own = jnp.where(slot == 0.0, here[0:2], here[2:4])
     halo = jnp.where(slot == 0.0, below[4:6], below[6:8])
     out_ref[...] = own + jnp.where(edge, halo, 0.0)
@@ -330,21 +365,35 @@
     noise = spectrum_noise.reshape(2, 8, 8, 64, 128).transpose(0, 1, 3, 2, 4).reshape(2, 8, 512, 128)
     power = power_spectrum.reshape(8, 8, 64, 128).transpose(0, 2, 1, 3).reshape(8, 512, 128)
     block = site_block.reshape(1, DEVICES)
+    operands = [
+        pltpu.with_memory_space_constraint(operand, pltpu.HBM)
+        for operand in map(
+            jnp.asarray,
+            (noise, power, block, site_cell, site_frac, short_first, turn_first, long_both),
+        )
+    ]
     sent = pl.pallas_call(
         first_kernel,
         out_shape=jax.ShapeDtypeStruct((DEVICES * MESSAGE, 128), jnp.float32),
-        in_specs=[any_space, any_space] + [VMEM] * 6,
+        in_specs=[pl.BlockSpec(memory_space=pltpu.HBM)] * 8,
         out_specs=VMEM,
         scratch_shapes=[
             pltpu.VMEM((2, 8, 512, 128), jnp.float32),
             pltpu.VMEM((8, 512, 128), jnp.float32),
-            pltpu.VMEM((2, 4096, 128), jnp.float32),
-            pltpu.SemaphoreType.DMA((8,)),
-            pltpu.SemaphoreType.DMA((8,)),
+            pltpu.VMEM((1, DEVICES), jnp.int32),
+            pltpu.VMEM((2, DEVICES), jnp.int32),
+            pltpu.VMEM((2, DEVICES), jnp.float32),
+            pltpu.VMEM((256, 256), jnp.bfloat16),
+            pltpu.VMEM((2, 64, 128), jnp.float32),
+            pltpu.VMEM((2, 256, 256), jnp.bfloat16),
+            pltpu.VMEM((2, 64 * PITCH, 128), jnp.float32),
+            pltpu.SemaphoreType.DMA((len(CHUNKS),)),
+            pltpu.SemaphoreType.DMA((len(CHUNKS),)),
+            pltpu.SemaphoreType.DMA((6,)),
         ],
         compiler_params=pltpu.CompilerParams(vmem_limit_bytes=40 << 20),
         name="first_pass",
-    )(noise, power, block, site_cell, site_frac, short_first, turn_first, long_both)
+    )(*operands)
     got = exchange(sent.reshape(DEVICES * MESSAGE, 1, 128)).reshape(DEVICES * MESSAGE, 128)
     field, answer = pl.pallas_call(
         second_kernel,
@@ -356,7 +405,7 @@
         out_specs=(any_space, VMEM),
         scratch_shapes=[
             pltpu.VMEM((2, 4096, 128), jnp.float32),
-            pltpu.VMEM((2, 2, 6, DEVICES, 128), jnp.float32),
+            pltpu.VMEM((2, 2, 3, DEVICES, 128), jnp.float32),
             pltpu.VMEM((DEVICES, 128), jnp.int32),
             pltpu.SMEM((DEVICES, 128), jnp.int32),
             pltpu.SemaphoreType.DMA((8,)),

time: 108 us -> 96.3 us (0.89)
  local copies, waits for them, and re-layouts: 8.49 us -> 0.02 us
  Pallas kernels: 19.2 us -> 15.8 us
    unnamed x20 -> x6, local copies, waits for them, and re-layouts: 8.49 us -> 0.02 us
    pallas_call x1, Pallas kernels: 9.51 us -> 6.31 us  [per_device(): pl.pallas_call(first_kernel, out_shape=jax.ShapeDtypeStruct((DEVICES * ME...]
where the time goes in v1:
time: 96.3 us; the launch traced here: 96.1 us
  blocking collectives  79.7 us (83%)
  Pallas kernels  15.8 us (16%)
    all_to_all x2, blocking collectives, exchange(): return lax.all_to_all(value, AXES, split_axis=0, concat_axis=0, tiled=True)  79.7 us
    pallas_call x1, Pallas kernels, per_device(): pl.pallas_call(second_kernel, out_shape=(jax.ShapeDtypeStruct((2, 4096, 1...  7.82 us
    pallas_call x1, Pallas kernels, per_device(): pl.pallas_call(first_kernel, out_shape=jax.ShapeDtypeStruct((DEVICES * ME...  6.31 us

profile of v1, /device:TPU:1, one launch (start us, length us, event | category | flops | bytes accessed | tf_op | source)
XLA Modules:
  0.0 96.1 jit_solution(17461528903421549690)
XLA Ops:
  0.6 6.3 %first_pass.1 = f32[8320,128]{1,0:T(8,128)S(1)} custom-call(f32[2,8,512,128]{3,2,1,0:T(8,128)} %bitcast.27, f32[8,512,128]{2,1,0:T(8,128)} %bitcast.28, s32[1,128]{1,0:T(1,128)} %bitcast.30, s32[2,128]{1,0:T(2,128)} %cell_ref.1, f32[2,128]{1,0:T(2,128)} %frac_hbm.1, bf16[256,256]{1,0:T(8,128)(2,1)} %constant.10.clone.short_hbm, ...), custom_call_target="tpu_custom_call" | custom-call | tf_op jit(solution)/shard_map/first_pass/pallas_call | solution.py:375
  7.0 0.0 copy-start
  7.0 0.0 copy-start.1
  7.0 0.0 copy-start.2
  7.0 65.3 %all_to_all.10 = f32[8320,1,128]{2,1,0:T(1,128)S(1)} all-to-all(f32[8320,1,128]{2,1,0:T(1,128)S(1)} %bitcast.25), channel_id=1, replica_groups=mesh['row'=16,'col'=8] {'row','col'}, dimensions={0} | all-to-all | bytes 8519680 | tf_op jit(solution)/shard_map/all_to_all | solution.py:359
  72.3 0.0 copy-done
  72.3 0.0 copy-done.1
  72.3 0.0 copy-done.2
  72.3 7.8 %second_pass.1 = (f32[2,4096,128]{2,1,0:T(8,128)}, f32[128,128]{1,0:T(8,128)S(1)}) custom-call(f32[8320,128]{1,0:T(8,128)S(1)} %bitcast.24, bf16[2,256,256]{2,1,0:T(8,128)(2,1)S(1)} %copy-done, f32[2,128,128]{2,1,0:T(8,128)S(1)} %copy-done.2, bf16[2,256,256]{2,1,0:T(8,128)(2,1)S(1)} %copy-done.1), custom_call_target="tpu_custom_call" | custom-call | tf_op jit(solution)/shard_map/second_pass/pallas_call | solution.py:398
  80.1 14.4 %all_to_all.11 = f32[128,1,128]{2,1,0:T(1,128)} all-to-all(f32[128,1,128]{2,1,0:T(1,128)S(1)} %bitcast.26), channel_id=1, replica_groups=mesh['row'=16,'col'=8] {'row','col'}, dimensions={0} | all-to-all | bytes 131072 | tf_op jit(solution)/shard_map/all_to_all | solution.py:359
  94.5 1.6 %samples.1 = f32[2,128]{1,0:T(2,128)} custom-call(f32[128,128]{1,0:T(8,128)} %bitcast.29, s32[1,128]{1,0:T(1,128)} %bitcast.31, s32[2,128]{1,0:T(2,128)} %cell_ref.1), custom_call_target="tpu_custom_call" | custom-call | tf_op jit(solution)/shard_map/samples/pallas_call | solution.py:418
Async XLA Ops:
  7.0 65.3 %copy-start = (bf16[2,256,256]{2,1,0:T(8,128)(2,1)S(1)}, bf16[2,256,256]{2,1,0:T(8,128)(2,1)}, u32[]{:S(2)}) copy-start(bf16[2,256,256]{2,1,0:T(8,128)(2,1)} %constant.12.clone.long_hbm.long_ref) | copy-start | bytes 786436
  7.0 65.3 %copy-start.1 = (bf16[2,256,256]{2,1,0:T(8,128)(2,1)S(1)}, bf16[2,256,256]{2,1,0:T(8,128)(2,1)}, u32[]{:S(2)}) copy-start(bf16[2,256,256]{2,1,0:T(8,128)(2,1)} %constant.14.clone.short_ref) | copy-start | bytes 786436
  7.0 65.3 %copy-start.2 = (f32[2,128,128]{2,1,0:T(8,128)S(1)}, f32[2,128,128]{2,1,0:T(8,128)}, u32[]{:S(2)}) copy-start(f32[2,128,128]{2,1,0:T(8,128)} %constant.13.clone.turn_ref) | copy-start | bytes 393220

commit v2 on v1

--- a/solution.py
+++ b/solution.py
@@ -12,7 +12,7 @@
 ROWS = 64
 MESSAGE = 65
 PITCH = 72
-CHUNKS = ((0, 1), (1, 1), (2, 2), (4, 4))
+CHUNKS = ((0, 2), (2, 3), (5, 3))
 AXES = ("row", "col")
 VMEM = pl.BlockSpec(memory_space=pltpu.VMEM)
 HIGH = lax.Precision.HIGHEST
@@ -79,20 +79,15 @@
     column_next = (column + 1) & (GRID - 1)
     part_row, part_col = frac[0:1], frac[1:2]
     edge = row == ROWS - 1
-    row_next = jnp.where(edge, row, row + 1)
-
-    def line(field_row, field_col):
-        return ((field_row >> 3) * 512 + (field_col >> 7) * 8 + (field_row & 7)).astype(jnp.float32)
-
+    tile = (column >> 7).astype(jnp.float32)
+    tile_next = (column_next >> 7).astype(jnp.float32)
+    line = row.astype(jnp.float32)
     lane = (column & 127).astype(jnp.float32)
     lane_next = (column_next & 127).astype(jnp.float32)
     lower = jnp.where(edge, 0.0, part_row)
-    zero = jnp.zeros_like(row)
     own = [
-        line(row, column),
-        line(row, column_next),
-        line(row_next, column),
-        line(row_next, column_next),
+        PITCH * tile + line,
+        PITCH * tile_next + line,
         lane,
         lane_next,
         (1 - part_row) * (1 - part_col),
@@ -101,8 +96,8 @@
         lower * part_col,
     ]
     halo = [
-        line(zero, column),
-        line(zero, column_next),
+        tile,
+        tile_next,
         lane,
         lane_next,
         part_row * (1 - part_col),
@@ -110,7 +105,7 @@
     ]
     blank = jnp.zeros((1, DEVICES), jnp.float32)
     groups = []
-    for at, values in ((0, own), (10, own), (20, halo), (26, halo)):
+    for at, values in ((0, own), (8, own), (16, halo), (22, halo)):
         lines = [blank] * at + values
         groups.append(jnp.concatenate(lines + [blank] * (DEVICES - len(lines)), axis=0))
     owner = lax.broadcasted_iota(jnp.int32, (DEVICES, DEVICES), 0)
@@ -235,6 +230,7 @@
     short_ref,
     field_hbm,
     answer_ref,
+    tiles,
     field,
     picked,
     code_vmem,
@@ -242,6 +238,8 @@
     field_sem,
     code_sem,
 ):
+    for part in range(2):
+        field[part, pl.ds(ROWS, 64, stride=PITCH), :] = jnp.zeros((64, 128), jnp.float32)
     asked = got_ref[pl.ds(MESSAGE - 1, DEVICES, stride=MESSAGE), :]
     code_vmem[...] = (asked + 0.5).astype(jnp.int32)
     code_copy = pltpu.make_async_copy(code_vmem, code_smem, code_sem)
@@ -282,29 +280,30 @@
                 for odd in range(2):
                     for k in range(2):
                         top = 128 * part + 64 * odd
-                        at = pl.ds(512 * i + 4 * half + 2 * k + odd, 64, stride=8)
-                        field[part, at, :] = sums[top : top + 64, 128 * k : 128 * k + 128]
-        span = pl.ds(512 * i, 512)
+                        row = 4 * half + 2 * k + odd
+                        value = sums[top : top + 64, 128 * k : 128 * k + 128]
+                        tiles[part, pl.ds(512 * i + row, 64, stride=8), :] = value
+                        field[part, pl.ds(8 * i + row, 64, stride=PITCH), :] = value
         copies.append(
-            pltpu.make_async_copy(field.at[:, span], field_hbm.at[:, span], field_sem.at[i])
+            pltpu.make_async_copy(
+                tiles.at[:, pl.ds(512 * i, 512)], field_hbm.at[:, i], field_sem.at[i]
+            )
         )
         copies[-1].start()
     code_copy.wait()
 
-    head = lax.broadcasted_iota(jnp.int32, (1, 128), 1) == 0
+    head = lax.broadcasted_iota(jnp.int32, (2, 128), 1) == 0
 
     def gather(device, carry):
         for which in range(2):
-            for k in range(3):
-                lane = 10 * which + 2 * k if k < 2 else 20 + 6 * which
-                line = code_smem[device, lane]
-                line_next = code_smem[device, lane + 1]
-                for part in range(2):
-                    picked[which, part, k, pl.ds(device, 1), :] = jnp.where(
-                        head,
-                        field[part, pl.ds(line_next, 1), :],
-                        field[part, pl.ds(line, 1), :],
-                    )
+            line = code_smem[device, 8 * which]
+            line_next = code_smem[device, 8 * which + 1]
+            for part in range(2):
+                picked[which, part, pl.ds(2 * device, 2), :] = jnp.where(
+                    head,
+                    field[part, pl.ds(line_next, 2), :],
+                    field[part, pl.ds(line, 2), :],
+                )
         return carry
 
     lax.fori_loop(0, DEVICES, gather, 0, unroll=8)
@@ -314,24 +313,37 @@
     def column(at):
         return asked[:, at : at + 1]
 
+    first_row = pl.ds(0, 64, stride=PITCH)
+    terms = split(jnp.concatenate([field[0, first_row, :], field[1, first_row, :]], axis=1))
+    places = lax.broadcasted_iota(jnp.int32, (DEVICES, 128), 1) & 63
+    places = places.astype(jnp.float32)
+    masks = [
+        jnp.where(places == column(16 + 6 * which + k), 1.0, 0.0).astype(jnp.bfloat16)
+        for k in range(2)
+        for which in range(2)
+    ]
+    beyond = dot(jnp.concatenate(masks, axis=0), jnp.concatenate(terms, axis=0))
     for which in range(2):
-        own, halo = 10 * which, 20 + 6 * which
-
-        def weights(lane, weight):
-            return jnp.where(lanes == column(lane), column(weight), 0.0) + jnp.where(
-                lanes == column(lane + 1), column(weight + 1), 0.0
-            )
-
-        upper = weights(own + 4, own + 6)
-        lower = weights(own + 4, own + 8)
-        edge = weights(halo + 2, halo + 4)
+        own, halo = 8 * which, 16 + 6 * which
+
+        def weight(lane, value):
+            return jnp.where(lanes == column(lane), column(value), 0.0)
+
+        upper = weight(own + 2, own + 4) + weight(own + 3, own + 5)
+        lower = weight(own + 2, own + 6) + weight(own + 3, own + 7)
+        edge, edge_next = weight(halo + 2, halo + 4), weight(halo + 3, halo + 5)
         for part in range(2):
-            value = upper * picked[which, part, 0] + lower * picked[which, part, 1]
+            value = upper * picked[which, part, pl.ds(0, DEVICES, stride=2), :]
+            value += lower * picked[which, part, pl.ds(1, DEVICES, stride=2), :]
             answer = jnp.where(
                 lanes == 2 * which + part, jnp.sum(value, axis=1, keepdims=True), answer
             )
-            beyond = jnp.sum(edge * picked[which, part, 2], axis=1, keepdims=True)
-            answer = jnp.where(lanes == 4 + 2 * which + part, beyond, answer)
+            span = slice(128 * part, 128 * part + 128)
+            value = edge * beyond[128 * which : 128 * which + 128, span]
+            value += edge_next * beyond[256 + 128 * which : 384 + 128 * which, span]
+            answer = jnp.where(
+                lanes == 4 + 2 * which + part, jnp.sum(value, axis=1, keepdims=True), answer
+            )
     answer_ref[...] = answer
     for copy in copies:
         copy.wait()
@@ -398,14 +410,15 @@
     field, answer = pl.pallas_call(
         second_kernel,
         out_shape=(
-            jax.ShapeDtypeStruct((2, 4096, 128), jnp.float32),
+            jax.ShapeDtypeStruct((2, 8, 512, 128), jnp.float32),
             jax.ShapeDtypeStruct((DEVICES, 128), jnp.float32),
         ),
         in_specs=[VMEM] * 4,
         out_specs=(any_space, VMEM),
         scratch_shapes=[
             pltpu.VMEM((2, 4096, 128), jnp.float32),
-            pltpu.VMEM((2, 2, 3, DEVICES, 128), jnp.float32),
+            pltpu.VMEM((2, 64 * PITCH, 128), jnp.float32),
+            pltpu.VMEM((2, 2, 2 * DEVICES, 128), jnp.float32),
             pltpu.VMEM((DEVICES, 128), jnp.int32),
             pltpu.SMEM((DEVICES, 128), jnp.int32),
             pltpu.SemaphoreType.DMA((8,)),

time: 96.3 us -> 95.6 us (level)
  no operation moved by 1% of the time
where the time goes in v2:
time: 95.6 us; the launch traced here: 95.4 us
  blocking collectives  79.7 us (83%)
  Pallas kernels  15 us (16%)
    all_to_all x2, blocking collectives, exchange(): return lax.all_to_all(value, AXES, split_axis=0, concat_axis=0, tiled=True)  79.7 us
    pallas_call x1, Pallas kernels, per_device(): pl.pallas_call(second_kernel, out_shape=(jax.ShapeDtypeStruct((2, 8, 512,...  7.35 us
    pallas_call x1, Pallas kernels, per_device(): pl.pallas_call(first_kernel, out_shape=jax.ShapeDtypeStruct((DEVICES * ME...  6.07 us

profile of v2, /device:TPU:1, one launch (start us, length us, event | category | flops | bytes accessed | tf_op | source)
XLA Modules:
  0.0 95.4 jit_solution(1963517641436513654)
XLA Ops:
  0.6 6.1 %first_pass.1 = f32[8320,128]{1,0:T(8,128)S(1)} custom-call(f32[2,8,512,128]{3,2,1,0:T(8,128)} %bitcast.27, f32[8,512,128]{2,1,0:T(8,128)} %bitcast.28, s32[1,128]{1,0:T(1,128)} %bitcast.30, s32[2,128]{1,0:T(2,128)} %cell_ref.1, f32[2,128]{1,0:T(2,128)} %frac_hbm.1, bf16[256,256]{1,0:T(8,128)(2,1)} %constant.10.clone.short_hbm, ...), custom_call_target="tpu_custom_call" | custom-call | tf_op jit(solution)/shard_map/first_pass/pallas_call | solution.py:387
  6.7 0.0 copy-start
  6.7 0.0 copy-start.1
  6.7 0.0 copy-start.2
  6.7 65.3 %all_to_all.10 = f32[8320,1,128]{2,1,0:T(1,128)S(1)} all-to-all(f32[8320,1,128]{2,1,0:T(1,128)S(1)} %bitcast.25), channel_id=1, replica_groups=mesh['row'=16,'col'=8] {'row','col'}, dimensions={0} | all-to-all | bytes 8519680 | tf_op jit(solution)/shard_map/all_to_all | solution.py:371
  72.0 0.0 copy-done
  72.0 0.0 copy-done.1
  72.0 0.0 copy-done.2
  72.0 7.3 %second_pass.1 = (f32[2,8,512,128]{3,2,1,0:T(8,128)}, f32[128,128]{1,0:T(8,128)S(1)}) custom-call(f32[8320,128]{1,0:T(8,128)S(1)} %bitcast.24, bf16[2,256,256]{2,1,0:T(8,128)(2,1)S(1)} %copy-done, f32[2,128,128]{2,1,0:T(8,128)S(1)} %copy-done.2, bf16[2,256,256]{2,1,0:T(8,128)(2,1)S(1)} %copy-done.1), custom_call_target="tpu_custom_call" | custom-call | tf_op jit(solution)/shard_map/second_pass/pallas_call | solution.py:410
  79.4 14.4 %all_to_all.11 = f32[128,1,128]{2,1,0:T(1,128)} all-to-all(f32[128,1,128]{2,1,0:T(1,128)S(1)} %bitcast.26), channel_id=1, replica_groups=mesh['row'=16,'col'=8] {'row','col'}, dimensions={0} | all-to-all | bytes 131072 | tf_op jit(solution)/shard_map/all_to_all | solution.py:371
  93.8 1.6 %samples.1 = f32[2,128]{1,0:T(2,128)} custom-call(f32[128,128]{1,0:T(8,128)} %bitcast.29, s32[1,128]{1,0:T(1,128)} %bitcast.31, s32[2,128]{1,0:T(2,128)} %cell_ref.1), custom_call_target="tpu_custom_call" | custom-call | tf_op jit(solution)/shard_map/samples/pallas_call | solution.py:431
Async XLA Ops:
  6.7 65.3 %copy-start = (bf16[2,256,256]{2,1,0:T(8,128)(2,1)S(1)}, bf16[2,256,256]{2,1,0:T(8,128)(2,1)}, u32[]{:S(2)}) copy-start(bf16[2,256,256]{2,1,0:T(8,128)(2,1)} %constant.12.clone.long_hbm.long_ref) | copy-start | bytes 786436
  6.7 65.3 %copy-start.1 = (bf16[2,256,256]{2,1,0:T(8,128)(2,1)S(1)}, bf16[2,256,256]{2,1,0:T(8,128)(2,1)}, u32[]{:S(2)}) copy-start(bf16[2,256,256]{2,1,0:T(8,128)(2,1)} %constant.14.clone.short_ref) | copy-start | bytes 786436
  6.7 65.3 %copy-start.2 = (f32[2,128,128]{2,1,0:T(8,128)S(1)}, f32[2,128,128]{2,1,0:T(8,128)}, u32[]{:S(2)}) copy-start(f32[2,128,128]{2,1,0:T(8,128)} %constant.13.clone.turn_ref) | copy-start | bytes 393220

commit v3 on v2

--- a/solution.py
+++ b/solution.py
@@ -62,7 +62,7 @@
 
 def split_dot(table, value, dims=(((1,), (0,)), ((), ()))):
     high, low = split(value)
-    return dot(table[0], high, dims) + dot(table[0], low, dims) + dot(table[1], high, dims)
+    return dot(table[0], low, dims) + dot(table[1], high, dims) + dot(table[0], high, dims)
 
 
 def site_slots(block):

time: 95.6 us -> 95.4 us (level)
  no operation moved by 1% of the time
where the time goes in v3:
time: 95.4 us; the launch traced here: 95.2 us
  blocking collectives  79.7 us (84%)
  Pallas kernels  14.9 us (16%)
    all_to_all x2, blocking collectives, exchange(): return lax.all_to_all(value, AXES, split_axis=0, concat_axis=0, tiled=True)  79.7 us
    pallas_call x1, Pallas kernels, per_device(): pl.pallas_call(second_kernel, out_shape=(jax.ShapeDtypeStruct((2, 8, 512,...  7.17 us
    pallas_call x1, Pallas kernels, per_device(): pl.pallas_call(first_kernel, out_shape=jax.ShapeDtypeStruct((DEVICES * ME...  6.07 us

profile of v3, /device:TPU:1, one launch (start us, length us, event | category | flops | bytes accessed | tf_op | source)
XLA Modules:
  0.0 95.2 jit_solution(5767986977972942033)
XLA Ops:
  0.6 6.1 %first_pass.1 = f32[8320,128]{1,0:T(8,128)S(1)} custom-call(f32[2,8,512,128]{3,2,1,0:T(8,128)} %bitcast.27, f32[8,512,128]{2,1,0:T(8,128)} %bitcast.28, s32[1,128]{1,0:T(1,128)} %bitcast.30, s32[2,128]{1,0:T(2,128)} %cell_ref.1, f32[2,128]{1,0:T(2,128)} %frac_hbm.1, bf16[256,256]{1,0:T(8,128)(2,1)} %constant.10.clone.short_hbm, ...), custom_call_target="tpu_custom_call" | custom-call | tf_op jit(solution)/shard_map/first_pass/pallas_call | solution.py:387
  6.7 0.0 copy-start
  6.7 0.0 copy-start.1
  6.7 0.0 copy-start.2
  6.7 65.3 %all_to_all.10 = f32[8320,1,128]{2,1,0:T(1,128)S(1)} all-to-all(f32[8320,1,128]{2,1,0:T(1,128)S(1)} %bitcast.25), channel_id=1, replica_groups=mesh['row'=16,'col'=8] {'row','col'}, dimensions={0} | all-to-all | bytes 8519680 | tf_op jit(solution)/shard_map/all_to_all | solution.py:371
  72.0 0.0 copy-done
  72.0 0.0 copy-done.1
  72.0 0.0 copy-done.2
  72.0 7.2 %second_pass.1 = (f32[2,8,512,128]{3,2,1,0:T(8,128)}, f32[128,128]{1,0:T(8,128)S(1)}) custom-call(f32[8320,128]{1,0:T(8,128)S(1)} %bitcast.24, bf16[2,256,256]{2,1,0:T(8,128)(2,1)S(1)} %copy-done, f32[2,128,128]{2,1,0:T(8,128)S(1)} %copy-done.2, bf16[2,256,256]{2,1,0:T(8,128)(2,1)S(1)} %copy-done.1), custom_call_target="tpu_custom_call" | custom-call | tf_op jit(solution)/shard_map/second_pass/pallas_call | solution.py:410
  79.2 14.4 %all_to_all.11 = f32[128,1,128]{2,1,0:T(1,128)} all-to-all(f32[128,1,128]{2,1,0:T(1,128)S(1)} %bitcast.26), channel_id=1, replica_groups=mesh['row'=16,'col'=8] {'row','col'}, dimensions={0} | all-to-all | bytes 131072 | tf_op jit(solution)/shard_map/all_to_all | solution.py:371
  93.6 1.6 %samples.1 = f32[2,128]{1,0:T(2,128)} custom-call(f32[128,128]{1,0:T(8,128)} %bitcast.29, s32[1,128]{1,0:T(1,128)} %bitcast.31, s32[2,128]{1,0:T(2,128)} %cell_ref.1), custom_call_target="tpu_custom_call" | custom-call | tf_op jit(solution)/shard_map/samples/pallas_call | solution.py:431
Async XLA Ops:
  6.7 65.3 %copy-start = (bf16[2,256,256]{2,1,0:T(8,128)(2,1)S(1)}, bf16[2,256,256]{2,1,0:T(8,128)(2,1)}, u32[]{:S(2)}) copy-start(bf16[2,256,256]{2,1,0:T(8,128)(2,1)} %constant.12.clone.long_hbm.long_ref) | copy-start | bytes 786436
  6.7 65.3 %copy-start.1 = (bf16[2,256,256]{2,1,0:T(8,128)(2,1)S(1)}, bf16[2,256,256]{2,1,0:T(8,128)(2,1)}, u32[]{:S(2)}) copy-start(bf16[2,256,256]{2,1,0:T(8,128)(2,1)} %constant.14.clone.short_ref) | copy-start | bytes 786436
  6.7 65.3 %copy-start.2 = (f32[2,128,128]{2,1,0:T(8,128)S(1)}, f32[2,128,128]{2,1,0:T(8,128)}, u32[]{:S(2)}) copy-start(f32[2,128,128]{2,1,0:T(8,128)} %constant.13.clone.turn_ref) | copy-start | bytes 393220

commit v4 on v3

--- a/solution.py
+++ b/solution.py
@@ -290,6 +290,40 @@
             )
         )
         copies[-1].start()
+    lanes = lax.broadcasted_iota(jnp.int32, (DEVICES, 128), 1).astype(jnp.float32)
+    answer = jnp.zeros((DEVICES, 128), jnp.float32)
+
+    def column(at):
+        return asked[:, at : at + 1]
+
+    first_row = pl.ds(0, 64, stride=PITCH)
+    terms = split(jnp.concatenate([field[0, first_row, :], field[1, first_row, :]], axis=1))
+    places = lax.broadcasted_iota(jnp.int32, (DEVICES, 128), 1) & 63
+    places = places.astype(jnp.float32)
+    masks = [
+        jnp.where(places == column(16 + 6 * which + k), 1.0, 0.0).astype(jnp.bfloat16)
+        for k in range(2)
+        for which in range(2)
+    ]
+    beyond = dot(jnp.concatenate(masks, axis=0), jnp.concatenate(terms, axis=0))
+
+    def weight(lane, value):
+        return jnp.where(lanes == column(lane), column(value), 0.0)
+
+    weights = []
+    for which in range(2):
+        own, halo = 8 * which, 16 + 6 * which
+        upper = weight(own + 2, own + 4) + weight(own + 3, own + 5)
+        lower = weight(own + 2, own + 6) + weight(own + 3, own + 7)
+        weights.append((upper, lower))
+        edge, edge_next = weight(halo + 2, halo + 4), weight(halo + 3, halo + 5)
+        for part in range(2):
+            span = slice(128 * part, 128 * part + 128)
+            value = edge * beyond[128 * which : 128 * which + 128, span]
+            value += edge_next * beyond[256 + 128 * which : 384 + 128 * which, span]
+            answer = jnp.where(
+                lanes == 4 + 2 * which + part, jnp.sum(value, axis=1, keepdims=True), answer
+            )
     code_copy.wait()
 
     head = lax.broadcasted_iota(jnp.int32, (2, 128), 1) == 0
@@ -307,42 +341,13 @@
         return carry
 
     lax.fori_loop(0, DEVICES, gather, 0, unroll=8)
-    lanes = lax.broadcasted_iota(jnp.int32, (DEVICES, 128), 1).astype(jnp.float32)
-    answer = jnp.zeros((DEVICES, 128), jnp.float32)
-
-    def column(at):
-        return asked[:, at : at + 1]
-
-    first_row = pl.ds(0, 64, stride=PITCH)
-    terms = split(jnp.concatenate([field[0, first_row, :], field[1, first_row, :]], axis=1))
-    places = lax.broadcasted_iota(jnp.int32, (DEVICES, 128), 1) & 63
-    places = places.astype(jnp.float32)
-    masks = [
-        jnp.where(places == column(16 + 6 * which + k), 1.0, 0.0).astype(jnp.bfloat16)
-        for k in range(2)
-        for which in range(2)
-    ]
-    beyond = dot(jnp.concatenate(masks, axis=0), jnp.concatenate(terms, axis=0))
     for which in range(2):
-        own, halo = 8 * which, 16 + 6 * which
-
-        def weight(lane, value):
-            return jnp.where(lanes == column(lane), column(value), 0.0)
-
-        upper = weight(own + 2, own + 4) + weight(own + 3, own + 5)
-        lower = weight(own + 2, own + 6) + weight(own + 3, own + 7)
-        edge, edge_next = weight(halo + 2, halo + 4), weight(halo + 3, halo + 5)
+        upper, lower = weights[which]
         for part in range(2):
             value = upper * picked[which, part, pl.ds(0, DEVICES, stride=2), :]
             value += lower * picked[which, part, pl.ds(1, DEVICES, stride=2), :]
             answer = jnp.where(
                 lanes == 2 * which + part, jnp.sum(value, axis=1, keepdims=True), answer
-            )
-            span = slice(128 * part, 128 * part + 128)
-            value = edge * beyond[128 * which : 128 * which + 128, span]
-            value += edge_next * beyond[256 + 128 * which : 384 + 128 * which, span]
-            answer = jnp.where(
-                lanes == 4 + 2 * which + part, jnp.sum(value, axis=1, keepdims=True), answer
             )
     answer_ref[...] = answer
     for copy in copies:

time: 95.4 us -> 94.9 us (level)
  no operation moved by 1% of the time
where the time goes in v4:
time: 94.9 us; the launch traced here: 94.7 us
  blocking collectives  79.7 us (84%)
  Pallas kernels  14.4 us (15%)
    all_to_all x2, blocking collectives, exchange(): return lax.all_to_all(value, AXES, split_axis=0, concat_axis=0, tiled=True)  79.7 us
    pallas_call x1, Pallas kernels, per_device(): pl.pallas_call(second_kernel, out_shape=(jax.ShapeDtypeStruct((2, 8, 512,...  6.67 us
    pallas_call x1, Pallas kernels, per_device(): pl.pallas_call(first_kernel, out_shape=jax.ShapeDtypeStruct((DEVICES * ME...  6.07 us

profile of v4, /device:TPU:1, one launch (start us, length us, event | category | flops | bytes accessed | tf_op | source)
XLA Modules:
  0.0 94.7 jit_solution(2406907964737652218)
XLA Ops:
  0.6 6.1 %first_pass.1 = f32[8320,128]{1,0:T(8,128)S(1)} custom-call(f32[2,8,512,128]{3,2,1,0:T(8,128)} %bitcast.27, f32[8,512,128]{2,1,0:T(8,128)} %bitcast.28, s32[1,128]{1,0:T(1,128)} %bitcast.30, s32[2,128]{1,0:T(2,128)} %cell_ref.1, f32[2,128]{1,0:T(2,128)} %frac_hbm.1, bf16[256,256]{1,0:T(8,128)(2,1)} %constant.10.clone.short_hbm, ...), custom_call_target="tpu_custom_call" | custom-call | tf_op jit(solution)/shard_map/first_pass/pallas_call | solution.py:392
  6.7 0.0 copy-start
  6.7 0.0 copy-start.1
  6.7 0.0 copy-start.2
  6.7 65.3 %all_to_all.10 = f32[8320,1,128]{2,1,0:T(1,128)S(1)} all-to-all(f32[8320,1,128]{2,1,0:T(1,128)S(1)} %bitcast.25), channel_id=1, replica_groups=mesh['row'=16,'col'=8] {'row','col'}, dimensions={0} | all-to-all | bytes 8519680 | tf_op jit(solution)/shard_map/all_to_all | solution.py:376
  72.0 0.0 copy-done
  72.0 0.0 copy-done.1
  72.0 0.0 copy-done.2
  72.0 6.7 %second_pass.1 = (f32[2,8,512,128]{3,2,1,0:T(8,128)}, f32[128,128]{1,0:T(8,128)S(1)}) custom-call(f32[8320,128]{1,0:T(8,128)S(1)} %bitcast.24, bf16[2,256,256]{2,1,0:T(8,128)(2,1)S(1)} %copy-done, f32[2,128,128]{2,1,0:T(8,128)S(1)} %copy-done.2, bf16[2,256,256]{2,1,0:T(8,128)(2,1)S(1)} %copy-done.1), custom_call_target="tpu_custom_call" | custom-call | tf_op jit(solution)/shard_map/second_pass/pallas_call | solution.py:415
  78.7 14.4 %all_to_all.11 = f32[128,1,128]{2,1,0:T(1,128)} all-to-all(f32[128,1,128]{2,1,0:T(1,128)S(1)} %bitcast.26), channel_id=1, replica_groups=mesh['row'=16,'col'=8] {'row','col'}, dimensions={0} | all-to-all | bytes 131072 | tf_op jit(solution)/shard_map/all_to_all | solution.py:376
  93.1 1.6 %samples.1 = f32[2,128]{1,0:T(2,128)} custom-call(f32[128,128]{1,0:T(8,128)} %bitcast.29, s32[1,128]{1,0:T(1,128)} %bitcast.31, s32[2,128]{1,0:T(2,128)} %cell_ref.1), custom_call_target="tpu_custom_call" | custom-call | tf_op jit(solution)/shard_map/samples/pallas_call | solution.py:436
Async XLA Ops:
  6.7 65.3 %copy-start = (bf16[2,256,256]{2,1,0:T(8,128)(2,1)S(1)}, bf16[2,256,256]{2,1,0:T(8,128)(2,1)}, u32[]{:S(2)}) copy-start(bf16[2,256,256]{2,1,0:T(8,128)(2,1)} %constant.12.clone.long_hbm.long_ref) | copy-start | bytes 786436
  6.7 65.3 %copy-start.1 = (bf16[2,256,256]{2,1,0:T(8,128)(2,1)S(1)}, bf16[2,256,256]{2,1,0:T(8,128)(2,1)}, u32[]{:S(2)}) copy-start(bf16[2,256,256]{2,1,0:T(8,128)(2,1)} %constant.14.clone.short_ref) | copy-start | bytes 786436
  6.7 65.3 %copy-start.2 = (f32[2,128,128]{2,1,0:T(8,128)S(1)}, f32[2,128,128]{2,1,0:T(8,128)}, u32[]{:S(2)}) copy-start(f32[2,128,128]{2,1,0:T(8,128)} %constant.13.clone.turn_ref) | copy-start | bytes 393220

commit v5 on v4

--- a/solution.py
+++ b/solution.py
@@ -340,7 +340,7 @@
                 )
         return carry
 
-    lax.fori_loop(0, DEVICES, gather, 0, unroll=8)
+    lax.fori_loop(0, DEVICES, gather, 0, unroll=32)
     for which in range(2):
         upper, lower = weights[which]
         for part in range(2):

time: 94.9 us -> 94.8 us (level)
  no operation moved by 1% of the time
where the time goes in v5:
time: 94.8 us; the launch traced here: 94.6 us
  blocking collectives  79.7 us (84%)
  Pallas kernels  14.3 us (15%)
    all_to_all x2, blocking collectives, exchange(): return lax.all_to_all(value, AXES, split_axis=0, concat_axis=0, tiled=True)  79.7 us
    pallas_call x1, Pallas kernels, per_device(): pl.pallas_call(second_kernel, out_shape=(jax.ShapeDtypeStruct((2, 8, 512,...  6.61 us
    pallas_call x1, Pallas kernels, per_device(): pl.pallas_call(first_kernel, out_shape=jax.ShapeDtypeStruct((DEVICES * ME...  6.07 us

profile of v5, /device:TPU:1, one launch (start us, length us, event | category | flops | bytes accessed | tf_op | source)
XLA Modules:
  0.0 94.6 jit_solution(390796793175942902)
XLA Ops:
  0.6 6.1 %first_pass.1 = f32[8320,128]{1,0:T(8,128)S(1)} custom-call(f32[2,8,512,128]{3,2,1,0:T(8,128)} %bitcast.27, f32[8,512,128]{2,1,0:T(8,128)} %bitcast.28, s32[1,128]{1,0:T(1,128)} %bitcast.30, s32[2,128]{1,0:T(2,128)} %cell_ref.1, f32[2,128]{1,0:T(2,128)} %frac_hbm.1, bf16[256,256]{1,0:T(8,128)(2,1)} %constant.10.clone.short_hbm, ...), custom_call_target="tpu_custom_call" | custom-call | tf_op jit(solution)/shard_map/first_pass/pallas_call | solution.py:392
  6.7 0.0 copy-start
  6.7 0.0 copy-start.1
  6.7 0.0 copy-start.2
  6.7 65.3 %all_to_all.10 = f32[8320,1,128]{2,1,0:T(1,128)S(1)} all-to-all(f32[8320,1,128]{2,1,0:T(1,128)S(1)} %bitcast.25), channel_id=1, replica_groups=mesh['row'=16,'col'=8] {'row','col'}, dimensions={0} | all-to-all | bytes 8519680 | tf_op jit(solution)/shard_map/all_to_all | solution.py:376
  72.0 0.0 copy-done
  72.0 0.0 copy-done.1
  72.0 0.0 copy-done.2
  72.0 6.6 %second_pass.1 = (f32[2,8,512,128]{3,2,1,0:T(8,128)}, f32[128,128]{1,0:T(8,128)S(1)}) custom-call(f32[8320,128]{1,0:T(8,128)S(1)} %bitcast.24, bf16[2,256,256]{2,1,0:T(8,128)(2,1)S(1)} %copy-done, f32[2,128,128]{2,1,0:T(8,128)S(1)} %copy-done.2, bf16[2,256,256]{2,1,0:T(8,128)(2,1)S(1)} %copy-done.1), custom_call_target="tpu_custom_call" | custom-call | tf_op jit(solution)/shard_map/second_pass/pallas_call | solution.py:415
  78.7 14.4 %all_to_all.11 = f32[128,1,128]{2,1,0:T(1,128)} all-to-all(f32[128,1,128]{2,1,0:T(1,128)S(1)} %bitcast.26), channel_id=1, replica_groups=mesh['row'=16,'col'=8] {'row','col'}, dimensions={0} | all-to-all | bytes 131072 | tf_op jit(solution)/shard_map/all_to_all | solution.py:376
  93.0 1.6 %samples.1 = f32[2,128]{1,0:T(2,128)} custom-call(f32[128,128]{1,0:T(8,128)} %bitcast.29, s32[1,128]{1,0:T(1,128)} %bitcast.31, s32[2,128]{1,0:T(2,128)} %cell_ref.1), custom_call_target="tpu_custom_call" | custom-call | tf_op jit(solution)/shard_map/samples/pallas_call | solution.py:436
Async XLA Ops:
  6.7 65.3 %copy-start = (bf16[2,256,256]{2,1,0:T(8,128)(2,1)S(1)}, bf16[2,256,256]{2,1,0:T(8,128)(2,1)}, u32[]{:S(2)}) copy-start(bf16[2,256,256]{2,1,0:T(8,128)(2,1)} %constant.12.clone.long_hbm.long_ref) | copy-start | bytes 786436
  6.7 65.3 %copy-start.1 = (bf16[2,256,256]{2,1,0:T(8,128)(2,1)S(1)}, bf16[2,256,256]{2,1,0:T(8,128)(2,1)}, u32[]{:S(2)}) copy-start(bf16[2,256,256]{2,1,0:T(8,128)(2,1)} %constant.14.clone.short_ref) | copy-start | bytes 786436
  6.7 65.3 %copy-start.2 = (f32[2,128,128]{2,1,0:T(8,128)S(1)}, f32[2,128,128]{2,1,0:T(8,128)}, u32[]{:S(2)}) copy-start(f32[2,128,128]{2,1,0:T(8,128)} %constant.13.clone.turn_ref) | copy-start | bytes 393220
